TPU v7x, 128 devices: a whole 4x4x4 slice. The times are simulated.
128 devices in a mesh: row: 8 (over z_hi, x), col: 16 (over y, z_lo, core).
Axes of the slice: x: 4, y: 4, z: 4 (z_hi: 2, z_lo: 2; z = z_hi * 2 + z_lo), core: 2. Of those that a mesh axis runs over, the one named last changes fastest.
Arguments:
- pixels_tokens: bfloat16 [4, 2304, 5120], P(None, 'col', 'row'), may hold values from -12 to 12, as said below
- ln_gain: float32 [5120], replicated, may hold values from 0.1 to 1.9
- ln_bias: float32 [5120], replicated, may hold values from -3 to 3
- w_qkv: bfloat16 [5120, 12288], P('col', 'row'), may hold values from -1 to 1, as said below
- w_out: bfloat16 [4096, 5120], P('col', 'row'), may hold values from -0.09375 to 0.09375
Outputs:
- block_out: bfloat16 [4, 2304, 5120], P(None, 'col', 'row')
Inputs may be any that keep to these rules, and one draw needn't show every extreme that they name: `pixels_tokens`: activations of order one. `w_qkv`: projection entries scaled by the width.
All inputs are finite; a program needn't handle non-finite values.
Results may differ from a plain program's by a relative error of at most 0.012.
The roundings to bfloat16 on the way count: a program that leaves them out, or rounds other values in their place, can miss the bound.
Values may be sent and summed in bfloat16 or wider, within the bound.
A program may use at most 128 MiB of HBM per device.

v0:
```python
import jax
import jax.numpy as jnp
from jax import lax
from jax.sharding import PartitionSpec as P

HDIM = 128


def layer_norm(values, ln_gain, ln_bias):
    floats = values.astype(jnp.float32)
    center = jnp.mean(floats, axis=-1, keepdims=True)
    spread = jnp.mean((floats - center) * (floats - center), axis=-1, keepdims=True)
    return ((floats - center) * lax.rsqrt(spread + 1e-06) * ln_gain + ln_bias).astype(jnp.bfloat16)


def attend_item(item):
    width = item.shape[1] // 3
    query = item[:, :width]
    keys = item[:, width : 2 * width]
    values = item[:, 2 * width :]
    blocks = query.reshape(4, item.shape[0] // 4, width)

    def one_block(rows):
        scores = jnp.einsum(
            "qd,kd->qk", rows, keys, preferred_element_type=jnp.float32
        ) * width ** (-0.5)
        peak = jnp.max(scores, axis=-1, keepdims=True)
        expo = jnp.exp(scores - peak)
        weights = (expo / jnp.sum(expo, axis=-1, keepdims=True)).astype(jnp.bfloat16)
        return jnp.dot(weights, values, preferred_element_type=jnp.float32).astype(jnp.bfloat16)

    return lax.map(one_block, blocks).reshape(item.shape[0], width)


def local(pixels_tokens, ln_gain, ln_bias, w_qkv, w_out):
    images, seq_col, width_row = pixels_tokens.shape
    col_count = lax.axis_size("col")
    per_head = 3 * HDIM
    head_row = w_qkv.shape[1] // per_head
    items = images * head_row // col_count
    whole = lax.all_gather(pixels_tokens, "row", axis=2, tiled=True)
    normed = layer_norm(whole, ln_gain, ln_bias).reshape(images * seq_col, whole.shape[2])
    columns = normed
    qkv = jnp.dot(
        columns,
        lax.all_gather(w_qkv, "col", axis=0, tiled=True),
        preferred_element_type=jnp.float32,
    ).astype(jnp.bfloat16)
    outgoing = qkv.reshape(images, seq_col, head_row, per_head).transpose(0, 2, 1, 3)
    outgoing = outgoing.reshape(col_count, items, seq_col, per_head).transpose(1, 0, 2, 3)
    received = lax.all_to_all(outgoing, "col", split_axis=1, concat_axis=2, tiled=True)
    count = received.shape[0]
    heads_out = lax.map(attend_item, received.reshape(count, -1, per_head))
    back_send = heads_out.reshape(items, col_count, seq_col, HDIM)
    returned = lax.all_to_all(back_send, "col", split_axis=1, concat_axis=0, tiled=True)
    mixed = (
        returned.reshape(images, head_row, seq_col, HDIM)
        .transpose(0, 2, 1, 3)
        .reshape(images, seq_col, head_row * HDIM)
    )
    gathered = lax.all_gather(mixed, "row", axis=2, tiled=True)
    flat_heads = gathered.reshape(images * seq_col, gathered.shape[2])
    columns = flat_heads
    projected = jnp.dot(
        columns,
        lax.all_gather(w_out, "col", axis=0, tiled=True),
        preferred_element_type=jnp.float32,
    )
    summed = pixels_tokens.astype(jnp.float32) + projected.reshape(images, seq_col, width_row)
    return summed.astype(jnp.bfloat16)


def solution(mesh):
    in_specs = (P(None, "col", "row"), P(), P(), P("col", "row"), P("col", "row"))
    out_specs = P(None, "col", "row")
    return jax.shard_map(local, mesh=mesh, in_specs=in_specs, out_specs=out_specs, check_vma=False)
```

profile of v0, /device:TPU:1, one launch (start us, length us, event | category | flops | bytes accessed | tf_op | source)
XLA Modules:
  0.0 370.4 jit_solution(12865089088305254845)
XLA Ops:
  6.5 0.0 all-gather.5.cloned.1.call-start
  6.5 0.7 all-gather.5.cloned.1.call-update
  7.3 0.0 all-gather.7.cloned.1.call-start
  7.3 0.7 all-gather.7.cloned.1.call-update
  8.0 0.0 all-gather.11.cloned.1.call-start
  8.1 0.7 all-gather.11.cloned.1.call-update
  8.7 89.4 %all-gather.5.cloned.1.call-done = bf16[4,144,5120]{2,1,0:T(8,128)(2,1)} async-done(((bf16[4,144,640]{2,1,0:T(8,128)(2,1)}), bf16[4,144,5120]{2,1,0:T(8,128)(2,1)}) %all-gather.5.cloned.1.call-update) | async-done | bytes 5898256 | tf_op jit(solution)/shard_map/all_gather | solution.py:41
  98.2 0.0 copy-start
  98.2 0.0 copy-start.2
  98.2 0.0 copy-start.3
  98.2 3.7 convert_reduce_fusion
  101.9 0.7 copy-done
  102.6 1.7 fusion.10
  104.2 0.0 copy-done.2
  104.3 0.0 copy-done.3
  104.3 6.0 %fusion.13 = bf16[4,144,5120]{2,1,0:T(8,128)(2,1)} fusion(bf16[4,144,5120]{2,1,0:T(8,128)(2,1)S(1)} %copy-done, f32[5120]{0:T(1024)S(1)} %copy-done.2, f32[5120]{0:T(1024)S(1)} %copy-done.3, f32[4,144]{1,0:T(4,128)S(1)} %add_rsqrt_fusion, f32[4,144]{1,0:T(4,128)S(1)} %broadcast_multiply_fusion), kind=kLoop, calls=%fused_computation.18 | loop fusion | flops 17694720 | bytes 11842048 | tf_op jit(solution)/shard_map/convert_element_type | solution.py:13
  110.2 74.9 %all-gather.7.cloned.1.call-done = bf16[5120,1536]{1,0:T(8,128)(2,1)} async-done(((bf16[320,1536]{1,0:T(8,128)(2,1)}), bf16[5120,1536]{1,0:T(8,128)(2,1)}) %all-gather.7.cloned.1.call-update) | async-done | bytes 15728656 | tf_op jit(solution)/shard_map/all_gather | solution.py:46
  185.2 14.4 %convolution_convert_fusion = bf16[576,1536]{1,0:T(8,128)(2,1)S(1)} fusion(bf16[576,5120]{1,0:T(8,128)(2,1)} %bitcast.45, bf16[5120,1536]{1,0:T(8,128)(2,1)} %all-gather.7.cloned.1.call-done), kind=kOutput, calls=%fused_computation.21 | convolution fusion | flops 9060581376 | bytes 23396352 | tf_op jit(solution)/shard_map/dot_general | solution.py:44
  199.6 0.5 reshape.54
  200.0 1.5 copy.8
  201.5 5.2 %all-to-all-start = ((bf16[1,16,144,384]{3,2,0,1:T(8,128)(2,1)}), bf16[1,16,144,384]{3,2,0,1:T(8,128)(2,1)S(1)}, u32[]{:S(2)}, u32[]{:S(2)}) async-start(bf16[1,16,144,384]{3,2,0,1:T(8,128)(2,1)} %bitcast.44), calls=%async_computation | async-start | bytes 3538944 | tf_op jit(solution)/shard_map/all_to_all | solution.py:51
  206.7 0.2 all-gather.9.cloned.1.call-start
  206.9 33.8 %all-to-all-done = bf16[1,16,144,384]{3,2,0,1:T(8,128)(2,1)S(1)} async-done(((bf16[1,16,144,384]{3,2,0,1:T(8,128)(2,1)}), bf16[1,16,144,384]{3,2,0,1:T(8,128)(2,1)S(1)}, u32[]{:S(2)}, u32[]{:S(2)}) %all-to-all-start) | async-done | bytes 1769504 | tf_op jit(solution)/shard_map/all_to_all | solution.py:51
  240.7 0.3 fusion.19
  241.0 0.0 copy-start.1
  241.0 14.0 %while.17 = (s32[]{:T(128)}, bf16[4,576,128]{2,1,0:T(8,128)(2,1)}, bf16[4,576,128]{2,1,0:T(8,128)(2,1)S(1)}, bf16[2304,128]{1,0:T(8,128)(2,1)S(1)}, bf16[2304,128]{1,0:T(8,128)(2,1)S(1)}, /*index=5*/s32[]{:T(128)}) while((s32[]{:T(128)}, bf16[4,576,128]{2,1,0:T(8,128)(2,1)}, bf16[4,576,128]{2,1,0:T(8,128)(2,1)S(1)}, ...), condition=%wide.region_5.0_spmd, body=%wide.region_2.5_spmd.sunk | while | flops 688839552 | bytes 17411912 | solution.py:32
  241.0 0.9 fusion.32
  242.0 0.9 fusion.33
  242.8 1.7 fusion.34
  244.5 0.9 fusion.32
  245.4 0.9 fusion.33
  246.3 1.7 fusion.34
  248.0 0.9 fusion.32
  248.9 0.9 fusion.33
  249.8 1.7 fusion.34
  251.5 0.9 fusion.32
  252.4 0.9 fusion.33
  253.3 1.7 fusion.34
  255.0 17.6 %all_to_all.8 = bf16[1,16,144,128]{3,2,0,1:T(8,128)(2,1)S(1)} all-to-all(bf16[1,16,144,128]{3,2,0,1:T(8,128)(2,1)} %bitcast.8), channel_id=1, replica_groups=mesh['row'=8,'col'=16] {'col'}, dimensions={1} | all-to-all | bytes 1179648 | tf_op jit(solution)/shard_map/all_to_all | solution.py:55
  272.6 0.9 copy.13
  273.5 0.0 all-gather.9.cloned.1.call-update
  273.5 0.0 all-gather.11.cloned.1.call-done
  273.5 81.7 %all-gather.9.cloned.1.call-done = bf16[4,144,4096]{2,1,0:T(8,128)(2,1)} async-done(((bf16[4,144,512]{2,1,0:T(8,128)(2,1)}), bf16[4,144,4096]{2,1,0:T(8,128)(2,1)}) %all-gather.9.cloned.1.call-update) | async-done | bytes 4718608 | tf_op jit(solution)/shard_map/all_gather | solution.py:61
  355.2 0.0 copy-done.1
  355.2 8.6 %add_convert_fusion = bf16[4,144,640]{2,1,0:T(8,128)(2,1)} fusion(bf16[4,144,640]{2,1,0:T(8,128)(2,1)S(1)} %copy-done.1, bf16[4,144,4096]{2,1,0:T(8,128)(2,1)} %all-gather.9.cloned.1.call-done, bf16[4096,640]{1,0:T(8,128)(2,1)} %all-gather.11.cloned.1.call-done), kind=kOutput, calls=%fused_computation.22 | convolution fusion | flops 3021004800 | bytes 11436032 | tf_op jit(solution)/shard_map/dot_general | solution.py:64
  (3 shorter events, 0.0 us)
Async XLA Ops:
  6.5 91.6 %all-gather.5.cloned.1.call-start = ((), (), s32[]{:S(2)}) async-start(), calls=%async_computation.2 | async-start | bytes 6635520 | tf_op jit(solution)/shard_map/all_gather | solution.py:41
  7.3 177.9 %all-gather.7.cloned.1.call-start = ((), (), s32[]{:S(2)}) async-start(), calls=%async_computation.3 | async-start | bytes 16711680 | tf_op jit(solution)/shard_map/all_gather | solution.py:46
  8.0 265.5 %all-gather.11.cloned.1.call-start = ((), (), s32[]{:S(2)}) async-start(), calls=%async_computation.5 | async-start | bytes 5570560 | tf_op jit(solution)/shard_map/all_gather | solution.py:66
  98.2 4.4 %copy-start = (bf16[4,144,5120]{2,1,0:T(8,128)(2,1)S(1)}, bf16[4,144,5120]{2,1,0:T(8,128)(2,1)}, u32[]{:S(2)}) copy-start(bf16[4,144,5120]{2,1,0:T(8,128)(2,1)} %all-gather.5.cloned.1.call-done) | copy-start | bytes 17694724
  98.2 6.1 %copy-start.2 = (f32[5120]{0:T(1024)S(1)}, f32[5120]{0:T(1024)}, u32[]{:S(2)}) copy-start(f32[5120]{0:T(1024)} %param.9) | copy-start | bytes 61444
  98.2 6.1 %copy-start.3 = (f32[5120]{0:T(1024)S(1)}, f32[5120]{0:T(1024)}, u32[]{:S(2)}) copy-start(f32[5120]{0:T(1024)} %param.8) | copy-start | bytes 61444
  201.5 39.2 %all-to-all-start = ((bf16[1,16,144,384]{3,2,0,1:T(8,128)(2,1)}), bf16[1,16,144,384]{3,2,0,1:T(8,128)(2,1)S(1)}, u32[]{:S(2)}, u32[]{:S(2)}) async-start(bf16[1,16,144,384]{3,2,0,1:T(8,128)(2,1)} %bitcast.44), calls=%async_computation | async-start | bytes 3538944 | tf_op jit(solution)/shard_map/all_to_all | solution.py:51
  206.7 148.6 %all-gather.9.cloned.1.call-start = ((), (), s32[]{:S(2)}) async-start(), calls=%async_computation.4 | async-start | bytes 5308416 | tf_op jit(solution)/shard_map/all_gather | solution.py:61
  241.0 114.2 %copy-start.1 = (bf16[4,144,640]{2,1,0:T(8,128)(2,1)S(1)}, bf16[4,144,640]{2,1,0:T(8,128)(2,1)}, u32[]{:S(2)}) copy-start(bf16[4,144,640]{2,1,0:T(8,128)(2,1)} %param.7) | copy-start | bytes 2211844
Sparse Core Ops, SparseCore 0:
  9.7 88.4 all-gather.4
  99.9 85.2 all-gather.6
  186.9 58.2 all-gather.10
  273.6 81.5 all-gather.8
where the time goes:
time: 371 us; the launch traced here: 370 us
  waiting for transfers between devices  282 us (76%)
  matrix products  33.5 us (9%)
  blocking collectives  17.6 us (5%)
  other arithmetic  14.8 us (4%)
  between operations  13.2 us (4%)
  starting transfers between devices  5.47 us (1%)
  local copies, waits for them, and re-layouts  3.84 us (1%)
    all_gather x1, waiting for transfers between devices, local(): whole = lax.all_gather(pixels_tokens, 'row', axis=2, tiled=True)  89.4 us
    all_gather x1, waiting for transfers between devices, local(): gathered = lax.all_gather(mixed, 'row', axis=2, tiled=True)  81.7 us
    all_gather x1, waiting for transfers between devices, local(): lax.all_gather(w_qkv, 'col', axis=0, tiled=True)  74.9 us
    all_to_all x1, waiting for transfers between devices, local(): lax.all_to_all(outgoing, 'col', split_axis=1, concat_axis=2, tiled=True)  33.8 us
    all_to_all x1, blocking collectives, local(): lax.all_to_all(back_send, 'col', split_axis=1, concat_axis=0, tiled=True)  17.6 us
    dot_general x1, matrix products, local(): jnp.dot(columns, lax.all_gather(w_qkv, 'col', axis=0, tiled=True), prefer...  14.4 us
    dot_general x1, matrix products, local(): jnp.dot(columns, lax.all_gather(w_out, 'col', axis=0, tiled=True), prefer...  8.61 us
  transfers between devices with their start and end apart: 5, of which 4 were waited for; matrix products, arithmetic and copies ran while one was open for 12% of the time, Pallas kernels for 0%

commit v1 on v0

v1 whole, which is shorter than its diff:
```python
import jax
import jax.numpy as jnp
from jax import lax
from jax.experimental import pallas as pl
from jax.experimental.pallas import tpu as pltpu
from jax.sharding import PartitionSpec as P

HDIM = 128
MESH = pl.DeviceIdType.MESH
HALVES = (0, 1)
OWN, A, BP, BM, CP, CM, D, E = range(8)


def ring(p, step):
    return lax.rem(p + step + 4, 4)


class Gather:
    def __init__(self, p, q, device, block, view, source, sems, last_by_pair, sibling=None):
        self.p, self.q, self.device, self.block = p, q, device, block
        self.view, self.source, self.sems = view, source, sems
        self.last_by_pair, self.sibling = last_by_pair, sibling
        self.sent = []

    def place(self, role):
        p, q, o = self.p, self.q, 1 - self.q
        return {
            OWN: (p, q), A: (p, o), BP: (ring(p, -1), q), BM: (ring(p, 1), q),
            CP: (ring(p, -1), o), CM: (ring(p, 1), o), D: (ring(p, 2), q), E: (ring(p, 2), o),
        }[role]

    def ref(self, role, half):
        return self.view(self.block(*self.place(role)), half)

    def send(self, role, half, there, to):
        send_sem, recv_sem = self.sems[0], self.sems[1]
        src = self.source(half) if role == OWN and self.source is not None else self.ref(role, half)
        copy = pltpu.make_async_remote_copy(
            src_ref=src,
            dst_ref=self.ref(role, half),
            send_sem=send_sem.at[there, half],
            recv_sem=recv_sem.at[there, half],
            device_id=to,
            device_id_type=MESH,
        )
        copy.start()
        self.sent.append(copy)

    def share(self, role, half):
        if self.sibling is None:
            return
        device, view = self.sibling
        send_sem, recv_sem = self.sems[2], self.sems[3]
        src = self.source(half) if role == OWN and self.source is not None else self.ref(role, half)
        copy = pltpu.make_async_remote_copy(
            src_ref=src,
            dst_ref=self.ref(role, half),
            send_sem=send_sem.at[role, half],
            recv_sem=recv_sem.at[role, half],
            device_id=device,
            device_id_type=MESH,
        )
        copy.start()
        self.sent.append(copy)

    def up(self):
        return self.device(ring(self.p, 1), self.q)

    def down(self):
        return self.device(ring(self.p, -1), self.q)

    def across(self):
        return self.device(self.p, 1 - self.q)

    def begin(self, half):
        self.send(OWN, half, A, self.across())
        self.send(OWN, half, BP, self.up())
        self.send(OWN, half, BM, self.down())
        self.share(OWN, half)

    def arrive(self, role, half):
        recv_sem = self.sems[1]
        here = self.ref(role, half)
        pltpu.make_async_copy(here, here, recv_sem.at[role, half]).wait()
        if role == A:
            self.send(A, half, CP, self.up())
            self.send(A, half, CM, self.down())
        elif role == BP and half == 0:
            self.send(BP, half, D, self.up())
        elif role == BM and half == 1:
            self.send(BM, half, D, self.down())
        elif role == D and self.last_by_pair:
            self.send(D, half, E, self.across())
        elif role == CP and half == 0 and not self.last_by_pair:
            self.send(CP, half, E, self.up())
        elif role == CM and half == 1 and not self.last_by_pair:
            self.send(CM, half, E, self.down())
        self.share(role, half)

    def shared(self, role):
        _, view = self.sibling
        for half in HALVES:
            here = view(self.place(role), half)
            pltpu.make_async_copy(here, here, self.sems[3].at[role, half]).wait()

    def finish(self):
        for copy in self.sent:
            copy.wait_send()


def block_kernel(
    x_ref, gain_ref, bias_ref, wq_ref, wo_ref, out_ref,
    xbuf, nbuf, wbuf, wobuf, acc, qkv, item, hout, hbuf, pacc,
    xs, xr, ws, wr, wss, wsr, os, orr, oss, osr, hs, hr,
    as_, ar, bs, br, local_sem,
):
    row, col = lax.axis_index("row"), lax.axis_index("col")
    zh, xx = lax.div(row, 4), lax.rem(row, 4)
    yy, zl, core = lax.div(col, 4), lax.rem(lax.div(col, 2), 2), lax.rem(col, 2)
    tokens, feat = x_ref.shape
    wrows, wcols = wq_ref.shape
    orows, ocols = wo_ref.shape
    seq_col = tokens // 4
    per_head = 3 * HDIM

    def col_device(y, z):
        return (row, y * 4 + z * 2 + core)

    def row_device(x, h):
        return (h * 4 + x, col)

    def col_peer(d):
        return lax.rem(col + d, 16)

    barrier = pltpu.get_barrier_semaphore()
    for d in range(1, 16):
        pl.semaphore_signal(barrier, inc=1, device_id=(row, col_peer(d)), device_id_type=MESH)
    for peer in (row_device(ring(xx, 1), zh), row_device(ring(xx, -1), zh), row_device(xx, 1 - zh)):
        pl.semaphore_signal(barrier, inc=1, device_id=peer, device_id_type=MESH)

    def cols(ref, start, size, rows=None):
        rows = pl.ds(0, tokens) if rows is None else rows
        return ref.at[rows, pl.ds(pl.multiple_of(start, 128), size)]

    def weight_view(buf, rows, k):
        half_rows = rows // 2

        def view(place, half):
            start = (place[0] * 4 + place[1] * 2 + k) * rows + half * half_rows
            return buf.at[pl.ds(pl.multiple_of(start, 16), half_rows)]

        return view

    def weight_gather(src, buf, sems, last_by_pair):
        rows = src.shape[0]
        return Gather(
            yy, zl, col_device, lambda y, z: (y, z), weight_view(buf, rows, core),
            lambda half: src.at[pl.ds(half * (rows // 2), rows // 2)], sems, last_by_pair,
            sibling=((row, yy * 4 + zl * 2 + 1 - core), weight_view(buf, rows, 1 - core)),
        )

    half_tokens = tokens // 2

    def row_gather(buf, width, source, sems, last_by_pair):
        return Gather(
            xx, zh, row_device, lambda x, h: h * 4 + x,
            lambda b, half: cols(buf, b * width, width, pl.ds(half * half_tokens, half_tokens)),
            source, sems, last_by_pair,
        )

    gx = row_gather(xbuf, feat, lambda half: x_ref.at[pl.ds(half * half_tokens, half_tokens)], (xs, xr), False)
    gw = weight_gather(wq_ref, wbuf, (ws, wr, wss, wsr), True)
    go = weight_gather(wo_ref, wobuf, (os, orr, oss, osr), False)
    gh = row_gather(hbuf, 4 * HDIM, None, (hs, hr), True)

    own = [
        pltpu.make_async_copy(x_ref, cols(xbuf, row * feat, feat), local_sem.at[0]),
        pltpu.make_async_copy(wq_ref, wbuf.at[pl.ds(pl.multiple_of(col * wrows, 16), wrows)], local_sem.at[1]),
        pltpu.make_async_copy(wo_ref, wobuf.at[pl.ds(pl.multiple_of(col * orows, 16), orows)], local_sem.at[2]),
    ]
    for copy in own:
        copy.start()
    pl.semaphore_wait(barrier, 18)

    for half in HALVES:
        gx.begin(half)
        gw.begin(half)
    for copy in own:
        copy.wait()
    for half in HALVES:
        for role in (BP, BM, A):
            gx.arrive(role, half)
        for role in (BP, BM):
            gw.arrive(role, half)
        gw.arrive(A, half)
    gw.arrive(D, 0)
    gw.arrive(D, 1)
    for half in HALVES:
        gx.arrive(CP, half)
        gx.arrive(CM, half)
    for role in (D, E):
        for half in HALVES:
            gx.arrive(role, half)

    width = xbuf.shape[1]

    @pl.loop(0, tokens // 16)
    def _(i):
        rows = pl.ds(pl.multiple_of(i * 16, 16), 16)
        floats = xbuf[rows, :].astype(jnp.float32)
        center = jnp.sum(floats, axis=-1, keepdims=True) * (1.0 / width)
        moved = floats - center
        spread = jnp.sum(moved * moved, axis=-1, keepdims=True) * (1.0 / width)
        nbuf[rows, :] = (moved * lax.rsqrt(spread + 1e-06) * gain_ref[...] + bias_ref[...]).astype(jnp.bfloat16)

    unit = 2 * wrows

    def product(place, columns):
        at = pl.multiple_of((place[0] * 2 + place[1]) * unit, 128)
        return jnp.dot(
            nbuf[:, pl.ds(at, unit)], wbuf[pl.ds(at, unit), columns], preferred_element_type=jnp.float32
        )

    def multiply(role, first=False):
        gw.shared(role)
        place = gw.place(role)

        @pl.loop(0, wcols // per_head)
        def _(j):
            columns = pl.ds(pl.multiple_of(j * per_head, 128), per_head)
            if first:
                acc[:, columns] = product(place, columns)
            else:
                acc[:, columns] += product(place, columns)

    multiply(OWN, first=True)
    multiply(A)
    multiply(BP)
    multiply(BM)
    gw.arrive(CP, 0)
    gw.arrive(CM, 0)
    multiply(D)
    gw.arrive(E, 0)
    gw.arrive(E, 1)
    gw.arrive(CP, 1)
    gw.arrive(CM, 1)
    multiply(E)
    multiply(CP)
    gw.shared(CM)

    def item_rows(c):
        return pl.ds(pl.multiple_of(c * seq_col, 16), seq_col)

    head = lax.rem(col, 4)
    for j in range(4):
        columns = pl.ds(j * per_head, per_head)
        qkv[:, columns] = (acc[:, columns] + product(gw.place(CM), columns)).astype(jnp.bfloat16)

    def to_attend(d):
        c = col_peer(d)
        src = qkv.at[item_rows(lax.div(c, 4)), pl.ds(pl.multiple_of(lax.rem(c, 4) * per_head, 128), per_head)]
        return src, (row, c)

    attending = []
    for d in range(1, 16):
        src, device = to_attend(d)
        copy = pltpu.make_async_remote_copy(
            src_ref=src, dst_ref=item.at[item_rows(col)], send_sem=as_.at[d], recv_sem=ar.at[d],
            device_id=device, device_id_type=MESH,
        )
        copy.start()
        attending.append(copy)
    src, _ = to_attend(0)
    mine = pltpu.make_async_copy(src, item.at[item_rows(col)], local_sem.at[0])
    mine.start()
    mine.wait()
    for d in range(1, 16):
        here = item.at[item_rows(lax.rem(col - d + 16, 16))]
        pltpu.make_async_copy(here, here, ar.at[d]).wait()

    for half in HALVES:
        go.begin(half)

    def back_view(c):
        return hbuf.at[item_rows(lax.div(c, 4)), pl.ds(pl.multiple_of((row * 4 + lax.rem(c, 4)) * HDIM, 128), HDIM)]

    def back(d):
        c = col_peer(d)
        return pltpu.make_async_remote_copy(
            src_ref=hout.at[item_rows(c)], dst_ref=back_view(col), send_sem=bs.at[d], recv_sem=br.at[d],
            device_id=(row, c), device_id_type=MESH,
        )

    scale = HDIM ** (-0.5)

    def attend(c):
        rows = item_rows(c)
        scores = lax.dot_general(
            item[rows, :HDIM], item[:, HDIM : 2 * HDIM], (((1,), (1,)), ((), ())),
            preferred_element_type=jnp.float32,
        )
        peak = jnp.max(scores, axis=-1, keepdims=True)
        expo = jnp.exp((scores - peak) * scale)
        total = jnp.sum(expo, axis=-1, keepdims=True)
        mixed = jnp.dot(expo.astype(jnp.bfloat16), item[:, 2 * HDIM :], preferred_element_type=jnp.float32)
        hout[rows, :] = (mixed / total).astype(jnp.bfloat16)

    @pl.loop(1, 16)
    def _(d):
        attend(col_peer(d))
        back(d).start()

    attend(col)
    mine = pltpu.make_async_copy(hout.at[item_rows(col)], back_view(col), local_sem.at[0])
    mine.start()
    for half in HALVES:
        for role in (BP, BM, A):
            go.arrive(role, half)
    mine.wait()
    for d in range(1, 16):
        here = back_view(lax.rem(col - d + 16, 16))
        pltpu.make_async_copy(here, here, br.at[d]).wait()

    for half in HALVES:
        gh.begin(half)
    for half in HALVES:
        for role in (CP, CM):
            go.arrive(role, half)
    for role in (D, E):
        for half in HALVES:
            go.arrive(role, half)
    for role in range(8):
        go.shared(role)

    def project(role, first=False):
        at = pl.multiple_of(gh.block(*gh.place(role)) * 4 * HDIM, 128)
        part = jnp.dot(
            hbuf[:, pl.ds(at, 4 * HDIM)], wobuf[pl.ds(at, 4 * HDIM), :], preferred_element_type=jnp.float32
        )
        if first:
            pacc[...] = part
        else:
            pacc[...] += part

    project(OWN, first=True)
    for half in HALVES:
        for role in (BP, BM, A):
            gh.arrive(role, half)
    for role in (BP, BM, A):
        project(role)
    gh.arrive(D, 0)
    gh.arrive(D, 1)
    project(D)
    for half in HALVES:
        gh.arrive(CP, half)
        gh.arrive(CM, half)
    project(CP)
    project(CM)
    gh.arrive(E, 0)
    gh.arrive(E, 1)
    at = pl.multiple_of(gh.block(*gh.place(E)) * 4 * HDIM, 128)
    part = jnp.dot(hbuf[:, pl.ds(at, 4 * HDIM)], wobuf[pl.ds(at, 4 * HDIM), :], preferred_element_type=jnp.float32)
    residual = xbuf[:, pl.ds(pl.multiple_of(row * feat, 128), feat)].astype(jnp.float32)
    out_ref[...] = (residual + (pacc[...] + part)).astype(jnp.bfloat16)

    for gather in (gx, gw, go, gh):
        gather.finish()
    for copy in attending:
        copy.wait_send()
    for d in range(1, 16):
        back(d).wait_send()


def local(pixels_tokens, ln_gain, ln_bias, w_qkv, w_out):
    images, seq_col, feat = pixels_tokens.shape
    tokens = images * seq_col
    rows, cols = lax.axis_size("row"), lax.axis_size("col")
    bf16, f32 = jnp.bfloat16, jnp.float32
    width = rows * feat
    wcols, ocols = w_qkv.shape[1], w_out.shape[1]
    heads = cols * w_out.shape[0]
    dma = pltpu.SemaphoreType.DMA
    any_space = pl.BlockSpec(memory_space=pl.ANY)
    vmem = pl.BlockSpec(memory_space=pltpu.VMEM)
    pairs = [dma((8, 2)), dma((8, 2))]
    out = pl.pallas_call(
        block_kernel,
        out_shape=jax.ShapeDtypeStruct((tokens, feat), bf16),
        in_specs=[any_space, vmem, vmem, any_space, any_space],
        out_specs=vmem,
        scratch_shapes=[
            pltpu.VMEM((tokens, width), bf16),
            pltpu.VMEM((tokens, width), bf16),
            pltpu.VMEM((width, wcols), bf16),
            pltpu.VMEM((heads, ocols), bf16),
            pltpu.VMEM((tokens, wcols), f32),
            pltpu.VMEM((tokens, wcols), bf16),
            pltpu.VMEM((cols * seq_col, 3 * HDIM), bf16),
            pltpu.VMEM((cols * seq_col, HDIM), bf16),
            pltpu.VMEM((tokens, heads), bf16),
            pltpu.VMEM((tokens, ocols), f32),
            *pairs, *pairs, *pairs, *pairs, *pairs, *pairs,
            dma((16,)), dma((16,)), dma((16,)), dma((16,)), dma((3,)),
        ],
        compiler_params=pltpu.CompilerParams(
            collective_id=0, has_side_effects=True, vmem_limit_bytes=60 * 2**20
        ),
        name="attention_block",
    )(pixels_tokens.reshape(tokens, feat), ln_gain.reshape(1, -1), ln_bias.reshape(1, -1), w_qkv, w_out)
    return out.reshape(images, seq_col, feat)


def solution(mesh):
    in_specs = (P(None, "col", "row"), P(), P(), P("col", "row"), P("col", "row"))
    out_specs = P(None, "col", "row")
    return jax.shard_map(local, mesh=mesh, in_specs=in_specs, out_specs=out_specs, check_vma=False)
```

time: 371 us -> 181 us (0.49)
  the two profiles are of different devices: /device:TPU:1 before, /device:TPU:32 now
where the time goes in v1:
time: 181 us
  Pallas kernels  179 us (99%)
  local copies, waits for them, and re-layouts  2.04 us (1%)
    pallas_call x1, Pallas kernels, local(): pl.pallas_call(block_kernel, out_shape=jax.ShapeDtypeStruct((tokens, feat...  179 us

profile of v1, /device:TPU:32, one launch (start us, length us, event | category | flops | bytes accessed | tf_op | source)
XLA Modules:
  0.0 180.6 jit_solution(3343356468838536404)
XLA Ops:
  0.0 178.5 %attention_block.1 = bf16[576,640]{1,0:T(8,128)(2,1)} custom-call(bf16[576,640]{1,0:T(8,128)(2,1)} %bitcast.5, f32[1,5120]{1,0:T(1,128)} %bitcast.6, f32[1,5120]{1,0:T(1,128)} %bitcast.7, bf16[320,1536]{1,0:T(8,128)(2,1)} %wq_ref.1, bf16[256,640]{1,0:T(8,128)(2,1)} %wo_ref.1), custom_call_target="tpu_custom_call" | custom-call | tf_op jit(solution)/shard_map/attention_block/pallas_call | solution.py:386
  178.5 2.0 %copy.7 = bf16[4,144,640]{2,1,0:T(8,128)(2,1)} copy(bf16[4,144,640]{2,1,0:T(8,128)(2,1)} %bitcast.4) | data formatting | bytes 1474560

commit v2 on v1

v2 whole, which is shorter than its diff:
```python
import jax
import jax.numpy as jnp
from jax import lax
from jax.experimental import pallas as pl
from jax.experimental.pallas import tpu as pltpu
from jax.sharding import PartitionSpec as P

HDIM = 128
MESH = pl.DeviceIdType.MESH
HALVES = (0, 1)
OWN, A, BP, BM, CP, CM, D, E = range(8)


def ring(p, step):
    return lax.rem(p + step + 4, 4)


class Gather:
    def __init__(self, p, q, device, block, view, source, sems, last_by_pair, sibling=None):
        self.p, self.q, self.device, self.block = p, q, device, block
        self.view, self.source, self.sems = view, source, sems
        self.last_by_pair, self.sibling = last_by_pair, sibling
        self.sent = []

    def place(self, role):
        p, q, o = self.p, self.q, 1 - self.q
        return {
            OWN: (p, q), A: (p, o), BP: (ring(p, -1), q), BM: (ring(p, 1), q),
            CP: (ring(p, -1), o), CM: (ring(p, 1), o), D: (ring(p, 2), q), E: (ring(p, 2), o),
        }[role]

    def ref(self, role, half):
        return self.view(self.block(*self.place(role)), half)

    def send(self, role, half, there, to):
        send_sem, recv_sem = self.sems[0], self.sems[1]
        src = self.source(half) if role == OWN and self.source is not None else self.ref(role, half)
        copy = pltpu.make_async_remote_copy(
            src_ref=src,
            dst_ref=self.ref(role, half),
            send_sem=send_sem.at[there, half],
            recv_sem=recv_sem.at[there, half],
            device_id=to,
            device_id_type=MESH,
        )
        copy.start()
        self.sent.append(copy)

    def share(self, role, half):
        if self.sibling is None:
            return
        device, view = self.sibling
        send_sem, recv_sem = self.sems[2], self.sems[3]
        src = self.source(half) if role == OWN and self.source is not None else self.ref(role, half)
        copy = pltpu.make_async_remote_copy(
            src_ref=src,
            dst_ref=self.ref(role, half),
            send_sem=send_sem.at[role, half],
            recv_sem=recv_sem.at[role, half],
            device_id=device,
            device_id_type=MESH,
        )
        copy.start()
        self.sent.append(copy)

    def up(self):
        return self.device(ring(self.p, 1), self.q)

    def down(self):
        return self.device(ring(self.p, -1), self.q)

    def across(self):
        return self.device(self.p, 1 - self.q)

    def begin(self, half):
        self.send(OWN, half, A, self.across())
        self.send(OWN, half, BP, self.up())
        self.send(OWN, half, BM, self.down())
        self.share(OWN, half)

    def arrive(self, role, half):
        recv_sem = self.sems[1]
        here = self.ref(role, half)
        pltpu.make_async_copy(here, here, recv_sem.at[role, half]).wait()
        if role == A:
            self.send(A, half, CP, self.up())
            self.send(A, half, CM, self.down())
        elif role == BP and half == 0:
            self.send(BP, half, D, self.up())
        elif role == BM and half == 1:
            self.send(BM, half, D, self.down())
        elif role == D and self.last_by_pair:
            self.send(D, half, E, self.across())
        elif role == CP and half == 0 and not self.last_by_pair:
            self.send(CP, half, E, self.up())
        elif role == CM and half == 1 and not self.last_by_pair:
            self.send(CM, half, E, self.down())
        self.share(role, half)

    def shared(self, role):
        _, view = self.sibling
        for half in HALVES:
            here = view(self.place(role), half)
            pltpu.make_async_copy(here, here, self.sems[3].at[role, half]).wait()

    def finish(self):
        for copy in self.sent:
            copy.wait_send()


def block_kernel(
    x_ref, gain_ref, bias_ref, wq_ref, wo_ref, out_ref,
    xbuf, nbuf, wbuf, wobuf, acc, qkv, item0, item1, hout0, hout1, heads0, heads1, pacc,
    stats, moments,
    xs, xr, ws, wr, wss, wsr, os, orr, oss, osr, hs0, hr0, hs1, hr1,
    as_, ar, ass, asr, bs, br, ms, mr, local_sem,
):
    row, col = lax.axis_index("row"), lax.axis_index("col")
    zh, xx = lax.div(row, 4), lax.rem(row, 4)
    yy, zl, core = lax.div(col, 4), lax.rem(lax.div(col, 2), 2), lax.rem(col, 2)
    plane = lax.div(col, 2)
    tokens, feat = x_ref.shape
    wrows, wcols = wq_ref.shape
    orows, ocols = wo_ref.shape
    seq_col = tokens // 4
    per_head = 3 * HDIM
    items, houts, heads = (item0, item1), (hout0, hout1), (heads0, heads1)
    sibling = (row, plane * 2 + 1 - core)

    def col_device(y, z):
        return (row, y * 4 + z * 2 + core)

    def row_device(x, h):
        return (h * 4 + x, col)

    def plane_peer(d):
        return lax.rem(plane + d, 8)

    def plane_device(p):
        return (row, p * 2 + core)

    def row_peer(d):
        return (lax.rem(row + d, 8), col)

    barrier = pltpu.get_barrier_semaphore()
    for d in range(1, 8):
        pl.semaphore_signal(barrier, inc=1, device_id=plane_device(plane_peer(d)), device_id_type=MESH)
        pl.semaphore_signal(barrier, inc=1, device_id=row_peer(d), device_id_type=MESH)
    pl.semaphore_signal(barrier, inc=1, device_id=sibling, device_id_type=MESH)

    def cols(ref, start, size, rows=None):
        rows = pl.ds(0, tokens) if rows is None else rows
        return ref.at[rows, pl.ds(pl.multiple_of(start, 128), size)]

    half_rows = wrows // 2

    def wq_view(k):
        def view(place, half):
            start = (place[0] * 4 + place[1] * 2 + k) * wrows + half * half_rows
            return wbuf.at[pl.ds(pl.multiple_of(start, 16), half_rows)]

        return view

    def wo_view(k):
        def view(place, half):
            start = (place[0] * 4 + place[1] * 2 + k) * HDIM
            return wobuf.at[half, pl.ds(pl.multiple_of(start, 16), HDIM)]

        return view

    def weight_gather(src, view, sems, last_by_pair):
        size = src.shape[0] // 2
        return Gather(
            yy, zl, col_device, lambda y, z: (y, z), view(core),
            lambda half: src.at[pl.ds(half * size, size)], sems, last_by_pair,
            sibling=(sibling, view(1 - core)),
        )

    half_tokens = tokens // 2

    def row_gather(buf, width, source, sems, last_by_pair):
        return Gather(
            xx, zh, row_device, lambda x, h: h * 4 + x,
            lambda b, half: cols(buf, b * width, width, pl.ds(half * half_tokens, half_tokens)),
            source, sems, last_by_pair,
        )

    gx = row_gather(xbuf, feat, lambda half: x_ref.at[pl.ds(half * half_tokens, half_tokens)], (xs, xr), False)
    gw = weight_gather(wq_ref, wq_view, (ws, wr, wss, wsr), True)
    go = weight_gather(wo_ref, wo_view, (os, orr, oss, osr), False)
    gh = [
        row_gather(heads0, 2 * HDIM, None, (hs0, hr0), True),
        row_gather(heads1, 2 * HDIM, None, (hs1, hr1), True),
    ]

    own = [
        pltpu.make_async_copy(x_ref, cols(xbuf, row * feat, feat), local_sem.at[0]),
        pltpu.make_async_copy(wq_ref, wbuf.at[pl.ds(pl.multiple_of(col * wrows, 16), wrows)], local_sem.at[1]),
        pltpu.make_async_copy(wo_ref.at[pl.ds(0, HDIM)], wo_view(core)((yy, zl), 0), local_sem.at[2]),
        pltpu.make_async_copy(wo_ref.at[pl.ds(HDIM, HDIM)], wo_view(core)((yy, zl), 1), local_sem.at[3]),
    ]
    for copy in own:
        copy.start()
    pl.semaphore_wait(barrier, 15)

    for half in HALVES:
        gx.begin(half)
        gw.begin(half)
    for copy in own:
        copy.wait()

    padded = moments.shape[0]
    moments[...] = jnp.zeros_like(moments)

    @pl.loop(0, tokens // 32)
    def _(i):
        rows = pl.ds(pl.multiple_of(i * 32, 32), 32)
        floats = xbuf[rows, pl.ds(pl.multiple_of(row * feat, 128), feat)].astype(jnp.float32)
        center = jnp.sum(floats, axis=-1, keepdims=True) * (1.0 / feat)
        moved = floats - center
        square = jnp.sum(moved * moved, axis=-1, keepdims=True)
        lane = lax.broadcasted_iota(jnp.int32, (32, 128), 1)
        moments[rows, :] = jnp.where(lane == 0, center, jnp.where(lane == 1, square, 0.0))

    stats[row] = moments[...].T[:8]
    told = []
    for d in range(1, 8):
        copy = pltpu.make_async_remote_copy(
            src_ref=stats.at[row], dst_ref=stats.at[row], send_sem=ms.at[d], recv_sem=mr.at[d],
            device_id=row_peer(d), device_id_type=MESH,
        )
        copy.start()
        told.append(copy)
    for item in items:
        item[:, 3 * HDIM :] = jnp.ones((item.shape[0], HDIM), jnp.bfloat16)

    for role in (BP, BM, A):
        gx.arrive(role, 0)
    for role in (BP, BM, A):
        gw.arrive(role, 0)
    for d in range(1, 8):
        here = stats.at[lax.rem(row - d + 8, 8)]
        pltpu.make_async_copy(here, here, mr.at[d]).wait()
    centers = stats[:, 0, :]
    mean = jnp.sum(centers, axis=0, keepdims=True) * (1.0 / 8)
    off = centers - mean
    square = jnp.sum(stats[:, 1, :], axis=0, keepdims=True) + jnp.sum(off * off, axis=0, keepdims=True) * feat
    rate = lax.rsqrt(square * (1.0 / (8 * feat)) + 1e-06)
    line = lax.broadcasted_iota(jnp.int32, (128, padded), 0)
    moments[...] = jnp.where(line == 0, mean, rate).T

    def normalise(role):
        columns = pl.ds(pl.multiple_of(gx.block(*gx.place(role)) * feat, 128), feat)
        gain, bias = gain_ref[:, columns], bias_ref[:, columns]

        @pl.loop(0, tokens // 32)
        def _(i):
            rows = pl.ds(pl.multiple_of(i * 32, 32), 32)
            floats = xbuf[rows, columns].astype(jnp.float32)
            nbuf[rows, columns] = (
                (floats - moments[rows, 0:1]) * moments[rows, 1:2] * gain + bias
            ).astype(jnp.bfloat16)

    normalise(OWN)
    for role in (BP, BM, A):
        gx.arrive(role, 1)
    for role in (BP, BM, A):
        gw.arrive(role, 1)
    gw.arrive(D, 0)
    gw.arrive(D, 1)
    normalise(BP)
    normalise(BM)
    for half in HALVES:
        gx.arrive(CP, half)
        gx.arrive(CM, half)
    normalise(A)
    for half in HALVES:
        gx.arrive(D, half)
    for role in (CP, CM, D):
        normalise(role)
    for half in HALVES:
        gx.arrive(E, half)
    normalise(E)

    unit = 2 * wrows

    def product(place, columns):
        at = pl.multiple_of((place[0] * 2 + place[1]) * unit, 128)
        return jnp.dot(
            nbuf[:, pl.ds(at, unit)], wbuf[pl.ds(at, unit), columns], preferred_element_type=jnp.float32
        )

    def multiply(role, first=False):
        gw.shared(role)
        place = gw.place(role)

        @pl.loop(0, wcols // per_head)
        def _(j):
            columns = pl.ds(pl.multiple_of(j * per_head, 128), per_head)
            if first:
                acc[:, columns] = product(place, columns)
            else:
                acc[:, columns] += product(place, columns)

    multiply(OWN, first=True)
    multiply(BP)
    multiply(BM)
    multiply(A)
    gw.arrive(CP, 0)
    gw.arrive(CM, 0)
    multiply(D)
    gw.arrive(E, 0)
    gw.arrive(CP, 1)
    gw.arrive(CM, 1)
    gw.arrive(E, 1)
    for role in (CP, CM, E):
        gw.shared(role)

    def rows_of(p):
        return pl.ds(pl.multiple_of(p * seq_col, 16), seq_col)

    def to_attend(wave, d):
        p = plane_peer(d)
        start = pl.multiple_of((lax.rem(p, 2) * 2 + wave) * per_head, 128)
        src = qkv.at[rows_of(lax.div(p, 2)), pl.ds(start, per_head)]
        dst = items[wave].at[rows_of(plane), pl.ds(0, per_head)]
        return src, dst, plane_device(p)

    attending = []

    def attend_send(wave):
        for z in range(2):
            columns = pl.ds((z * 2 + wave) * per_head, per_head)
            total = acc[:, columns]
            for role in (CP, CM, E):
                total += product(gw.place(role), columns)
            qkv[:, columns] = total.astype(jnp.bfloat16)
        src, dst, _ = to_attend(wave, 0)
        mine = pltpu.make_async_copy(src, dst, local_sem.at[wave])
        mine.start()
        for d in range(1, 8):
            src, dst, device = to_attend(wave, d)
            copy = pltpu.make_async_remote_copy(
                src_ref=src, dst_ref=dst, send_sem=as_.at[wave, d], recv_sem=ar.at[wave, d],
                device_id=device, device_id_type=MESH,
            )
            copy.start()
            attending.append(copy)
        return mine

    both = pl.ds(HDIM, 2 * HDIM)

    def keys_share(wave, d):
        p = lax.rem(plane - d + 8, 8)
        copy = pltpu.make_async_remote_copy(
            src_ref=items[wave].at[rows_of(p), both], dst_ref=items[wave].at[rows_of(p + 8), both],
            send_sem=ass.at[wave, d], recv_sem=asr.at[wave, d],
            device_id=sibling, device_id_type=MESH,
        )
        copy.start()
        attending.append(copy)

    def attend_receive(wave, mine):
        mine.wait()
        keys_share(wave, 0)
        for d in range(1, 8):
            here = items[wave].at[rows_of(lax.rem(plane - d + 8, 8)), pl.ds(0, per_head)]
            pltpu.make_async_copy(here, here, ar.at[wave, d]).wait()
            keys_share(wave, d)
        for d in range(8):
            here = items[wave].at[rows_of(lax.rem(plane - d + 8, 8) + 8), both]
            pltpu.make_async_copy(here, here, asr.at[wave, d]).wait()

    def back_view(wave, p):
        start = pl.multiple_of(row * 2 * HDIM + lax.rem(p, 2) * HDIM, 128)
        return heads[wave].at[rows_of(lax.div(p, 2)), pl.ds(start, HDIM)]

    def back(wave, d):
        p = plane_peer(d)
        return pltpu.make_async_remote_copy(
            src_ref=houts[wave].at[rows_of(p)], dst_ref=back_view(wave, plane),
            send_sem=bs.at[wave, d], recv_sem=br.at[wave, d],
            device_id=plane_device(p), device_id_type=MESH,
        )

    power = HDIM ** (-0.5) * 1.4426950408889634

    def attend(wave, d):
        item, rows = items[wave], rows_of(plane_peer(d))
        scores = lax.dot_general(
            item[rows, :HDIM], item[:, HDIM : 2 * HDIM], (((1,), (1,)), ((), ())),
            preferred_element_type=jnp.float32,
        )
        peak = jnp.max(scores, axis=-1, keepdims=True)
        expo = jnp.exp2((scores - peak) * power).astype(jnp.bfloat16)
        mixed = jnp.dot(expo, item[:, 2 * HDIM :], preferred_element_type=jnp.float32)
        houts[wave][rows, :] = (mixed[:, :HDIM] / mixed[:, HDIM:]).astype(jnp.bfloat16)

    def attention(wave):
        for group in range(2):
            order = range(4 * group + 1, 4 * group + 5)
            for d in order:
                attend(wave, d)
            for d in order:
                if d < 8:
                    back(wave, d).start()
        mine = pltpu.make_async_copy(houts[wave].at[rows_of(plane)], back_view(wave, plane), local_sem.at[2])
        mine.start()
        mine.wait()

    def back_receive(wave):
        for d in range(1, 8):
            here = back_view(wave, lax.rem(plane - d + 8, 8))
            pltpu.make_async_copy(here, here, br.at[wave, d]).wait()
        for half in HALVES:
            gh[wave].begin(half)

    mine0 = attend_send(0)
    mine1 = attend_send(1)
    attend_receive(0, mine0)
    attention(0)
    back_receive(0)
    attend_receive(1, mine1)
    for half in HALVES:
        go.begin(half)
    attention(1)
    back_receive(1)

    def near(gather, half):
        for role in (BP, BM, A):
            gather.arrive(role, half)

    near(gh[0], 0)
    near(go, 0)
    near(gh[0], 1)
    near(go, 1)
    gh[0].arrive(D, 0)
    gh[0].arrive(D, 1)
    near(gh[1], 0)
    for half in HALVES:
        go.arrive(CP, half)
        go.arrive(CM, half)
    near(gh[1], 1)
    gh[1].arrive(D, 0)
    gh[1].arrive(D, 1)
    for role in (D, E):
        for half in HALVES:
            go.arrive(role, half)
    for role in range(8):
        go.shared(role)

    def part(wave, role):
        at = pl.multiple_of(gh[wave].block(*gh[wave].place(role)) * 2 * HDIM, 128)
        return jnp.dot(
            heads[wave][:, pl.ds(at, 2 * HDIM)], wobuf[wave, pl.ds(at, 2 * HDIM), :],
            preferred_element_type=jnp.float32,
        )

    def project(*terms):
        total = pacc[...]
        for wave, role in terms:
            total += part(wave, role)
        pacc[...] = total

    pacc[...] = xbuf[:, pl.ds(pl.multiple_of(row * feat, 128), feat)].astype(jnp.float32)
    project((0, OWN), (0, BP), (0, BM), (0, A), (0, D))
    for half in HALVES:
        for role in (CP, CM, E):
            gh[0].arrive(role, half)
    project((0, CP), (0, CM), (0, E), (1, OWN), (1, BP), (1, BM), (1, A), (1, D))
    for half in HALVES:
        for role in (CP, CM, E):
            gh[1].arrive(role, half)
    out_ref[...] = (pacc[...] + part(1, CP) + part(1, CM) + part(1, E)).astype(jnp.bfloat16)

    for gather in (gx, gw, go, *gh):
        gather.finish()
    for copy in told + attending:
        copy.wait_send()
    for wave in range(2):
        for d in range(1, 8):
            back(wave, d).wait_send()


def local(pixels_tokens, ln_gain, ln_bias, w_qkv, w_out):
    images, seq_col, feat = pixels_tokens.shape
    tokens = images * seq_col
    rows, cols = lax.axis_size("row"), lax.axis_size("col")
    bf16, f32 = jnp.bfloat16, jnp.float32
    width = rows * feat
    wcols, ocols = w_qkv.shape[1], w_out.shape[1]
    heads = cols * w_out.shape[0]
    dma = pltpu.SemaphoreType.DMA
    any_space = pl.BlockSpec(memory_space=pl.ANY)
    vmem = pl.BlockSpec(memory_space=pltpu.VMEM)
    pairs = [dma((8, 2)), dma((8, 2))]
    padded = -(-tokens // 128) * 128
    out = pl.pallas_call(
        block_kernel,
        out_shape=jax.ShapeDtypeStruct((tokens, feat), bf16),
        in_specs=[any_space, vmem, vmem, any_space, any_space],
        out_specs=vmem,
        scratch_shapes=[
            pltpu.VMEM((tokens, width), bf16),
            pltpu.VMEM((tokens, width), bf16),
            pltpu.VMEM((width, wcols), bf16),
            pltpu.VMEM((2, heads // 2, ocols), bf16),
            pltpu.VMEM((tokens, wcols), f32),
            pltpu.VMEM((tokens, wcols), bf16),
            pltpu.VMEM((cols * seq_col, 4 * HDIM), bf16),
            pltpu.VMEM((cols * seq_col, 4 * HDIM), bf16),
            pltpu.VMEM((cols * seq_col // 2, HDIM), bf16),
            pltpu.VMEM((cols * seq_col // 2, HDIM), bf16),
            pltpu.VMEM((tokens, heads // 2), bf16),
            pltpu.VMEM((tokens, heads // 2), bf16),
            pltpu.VMEM((tokens, ocols), f32),
            pltpu.VMEM((rows, 8, padded), f32),
            pltpu.VMEM((padded, 128), f32),
            *pairs, *pairs, *pairs, *pairs, *pairs, *pairs, *pairs,
            dma((2, 8)), dma((2, 8)), dma((2, 8)), dma((2, 8)), dma((2, 8)), dma((2, 8)),
            dma((8,)), dma((8,)), dma((4,)),
        ],
        compiler_params=pltpu.CompilerParams(
            collective_id=0, has_side_effects=True, vmem_limit_bytes=61 * 2**20
        ),
        name="attention_block",
    )(pixels_tokens.reshape(tokens, feat), ln_gain.reshape(1, -1), ln_bias.reshape(1, -1), w_qkv, w_out)
    return out.reshape(images, seq_col, feat)


def solution(mesh):
    in_specs = (P(None, "col", "row"), P(), P(), P("col", "row"), P("col", "row"))
    out_specs = P(None, "col", "row")
    return jax.shard_map(local, mesh=mesh, in_specs=in_specs, out_specs=out_specs, check_vma=False)
```

time: 181 us -> 181 us (level)
  the two profiles are of different devices: /device:TPU:32 before, /device:TPU:1 now
where the time goes in v2:
time: 181 us
  Pallas kernels  179 us (99%)
  local copies, waits for them, and re-layouts  2.04 us (1%)
    pallas_call x1, Pallas kernels, local(): pl.pallas_call(block_kernel, out_shape=jax.ShapeDtypeStruct((tokens, feat...  179 us

profile of v2, /device:TPU:1, one launch (start us, length us, event | category | flops | bytes accessed | tf_op | source)
XLA Modules:
  0.0 180.9 jit_solution(2660936704494380689)
XLA Ops:
  0.0 178.9 %attention_block.1 = bf16[576,640]{1,0:T(8,128)(2,1)} custom-call(bf16[576,640]{1,0:T(8,128)(2,1)} %bitcast.5, f32[1,5120]{1,0:T(1,128)} %bitcast.6, f32[1,5120]{1,0:T(1,128)} %bitcast.7, bf16[320,1536]{1,0:T(8,128)(2,1)} %wq_ref.1, bf16[256,640]{1,0:T(8,128)(2,1)} %wo_ref.1), custom_call_target="tpu_custom_call" | custom-call | tf_op jit(solution)/shard_map/attention_block/pallas_call | solution.py:498
  178.9 2.0 %copy.7 = bf16[4,144,640]{2,1,0:T(8,128)(2,1)} copy(bf16[4,144,640]{2,1,0:T(8,128)(2,1)} %bitcast.4) | data formatting | bytes 1474560

commit v3 on v2

--- a/solution.py
+++ b/solution.py
@@ -72,11 +72,17 @@
     def across(self):
         return self.device(self.p, 1 - self.q)
 
-    def begin(self, half):
+    def begin_across(self, half):
         self.send(OWN, half, A, self.across())
+
+    def begin_ring(self, half):
         self.send(OWN, half, BP, self.up())
         self.send(OWN, half, BM, self.down())
         self.share(OWN, half)
+
+    def begin(self, half):
+        self.begin_across(half)
+        self.begin_ring(half)
 
     def arrive(self, role, half):
         recv_sem = self.sems[1]
@@ -205,24 +211,26 @@
 
     for half in HALVES:
         gx.begin(half)
-        gw.begin(half)
+        gw.begin_ring(half)
     for copy in own:
         copy.wait()
 
-    padded = moments.shape[0]
-    moments[...] = jnp.zeros_like(moments)
-
-    @pl.loop(0, tokens // 32)
+    chunk = 96
+    means, rates = moments.at[0], moments.at[1]
+    padded = moments.shape[1]
+    means[...] = jnp.zeros_like(means)
+
+    @pl.loop(0, tokens // chunk)
     def _(i):
-        rows = pl.ds(pl.multiple_of(i * 32, 32), 32)
+        rows = pl.ds(pl.multiple_of(i * chunk, chunk), chunk)
         floats = xbuf[rows, pl.ds(pl.multiple_of(row * feat, 128), feat)].astype(jnp.float32)
         center = jnp.sum(floats, axis=-1, keepdims=True) * (1.0 / feat)
         moved = floats - center
         square = jnp.sum(moved * moved, axis=-1, keepdims=True)
-        lane = lax.broadcasted_iota(jnp.int32, (32, 128), 1)
-        moments[rows, :] = jnp.where(lane == 0, center, jnp.where(lane == 1, square, 0.0))
-
-    stats[row] = moments[...].T[:8]
+        lane = lax.broadcasted_iota(jnp.int32, (chunk, 128), 1)
+        means[rows, :] = jnp.where(lane == 0, center, jnp.where(lane == 1, square, 0.0))
+
+    stats[row] = means[...].T[:8]
     told = []
     for d in range(1, 8):
         copy = pltpu.make_async_remote_copy(
@@ -234,10 +242,10 @@
     for item in items:
         item[:, 3 * HDIM :] = jnp.ones((item.shape[0], HDIM), jnp.bfloat16)
 
-    for role in (BP, BM, A):
-        gx.arrive(role, 0)
-    for role in (BP, BM, A):
-        gw.arrive(role, 0)
+    gx.arrive(A, 0)
+    gw.begin_across(0)
+    gx.arrive(BP, 0)
+    gx.arrive(BM, 0)
     for d in range(1, 8):
         here = stats.at[lax.rem(row - d + 8, 8)]
         pltpu.make_async_copy(here, here, mr.at[d]).wait()
@@ -246,40 +254,50 @@
     off = centers - mean
     square = jnp.sum(stats[:, 1, :], axis=0, keepdims=True) + jnp.sum(off * off, axis=0, keepdims=True) * feat
     rate = lax.rsqrt(square * (1.0 / (8 * feat)) + 1e-06)
-    line = lax.broadcasted_iota(jnp.int32, (128, padded), 0)
-    moments[...] = jnp.where(line == 0, mean, rate).T
+    means[...] = jnp.broadcast_to(mean, (128, padded)).T
+    rates[...] = jnp.broadcast_to(rate, (128, padded)).T
 
     def normalise(role):
-        columns = pl.ds(pl.multiple_of(gx.block(*gx.place(role)) * feat, 128), feat)
-        gain, bias = gain_ref[:, columns], bias_ref[:, columns]
-
-        @pl.loop(0, tokens // 32)
+        start = gx.block(*gx.place(role)) * feat
+
+        @pl.loop(0, tokens // chunk)
         def _(i):
-            rows = pl.ds(pl.multiple_of(i * 32, 32), 32)
-            floats = xbuf[rows, columns].astype(jnp.float32)
-            nbuf[rows, columns] = (
-                (floats - moments[rows, 0:1]) * moments[rows, 1:2] * gain + bias
-            ).astype(jnp.bfloat16)
+            rows = pl.ds(pl.multiple_of(i * chunk, chunk), chunk)
+            mean, rate = means[rows, :], rates[rows, :]
+            for step in range(feat // 128):
+                columns = pl.ds(pl.multiple_of(start + step * 128, 128), 128)
+                floats = xbuf[rows, columns].astype(jnp.float32)
+                nbuf[rows, columns] = (
+                    (floats - mean) * rate * gain_ref[:, columns] + bias_ref[:, columns]
+                ).astype(jnp.bfloat16)
 
     normalise(OWN)
-    for role in (BP, BM, A):
-        gx.arrive(role, 1)
-    for role in (BP, BM, A):
-        gw.arrive(role, 1)
+    gw.arrive(BP, 0)
+    gw.arrive(BM, 0)
+    gx.arrive(A, 1)
+    gw.begin_across(1)
+    gx.arrive(BP, 1)
+    gx.arrive(BM, 1)
+    normalise(A)
+    normalise(BP)
+    normalise(BM)
+    gw.arrive(BP, 1)
+    gw.arrive(BM, 1)
+    gw.arrive(A, 0)
+    gx.arrive(CP, 0)
+    gx.arrive(CM, 0)
     gw.arrive(D, 0)
     gw.arrive(D, 1)
-    normalise(BP)
-    normalise(BM)
-    for half in HALVES:
-        gx.arrive(CP, half)
-        gx.arrive(CM, half)
-    normalise(A)
-    for half in HALVES:
-        gx.arrive(D, half)
-    for role in (CP, CM, D):
-        normalise(role)
-    for half in HALVES:
-        gx.arrive(E, half)
+    gw.arrive(A, 1)
+    gx.arrive(CP, 1)
+    gx.arrive(CM, 1)
+    normalise(CP)
+    normalise(CM)
+    gx.arrive(D, 0)
+    gx.arrive(D, 1)
+    normalise(D)
+    gx.arrive(E, 0)
+    gx.arrive(E, 1)
     normalise(E)
 
     unit = 2 * wrows
@@ -328,13 +346,15 @@
 
     attending = []
 
-    def attend_send(wave):
+    def complete(wave):
         for z in range(2):
             columns = pl.ds((z * 2 + wave) * per_head, per_head)
             total = acc[:, columns]
             for role in (CP, CM, E):
                 total += product(gw.place(role), columns)
             qkv[:, columns] = total.astype(jnp.bfloat16)
+
+    def attend_send(wave):
         src, dst, _ = to_attend(wave, 0)
         mine = pltpu.make_async_copy(src, dst, local_sem.at[wave])
         mine.start()
@@ -396,17 +416,17 @@
         mixed = jnp.dot(expo, item[:, 2 * HDIM :], preferred_element_type=jnp.float32)
         houts[wave][rows, :] = (mixed[:, :HDIM] / mixed[:, HDIM:]).astype(jnp.bfloat16)
 
-    def attention(wave):
-        for group in range(2):
-            order = range(4 * group + 1, 4 * group + 5)
-            for d in order:
-                attend(wave, d)
-            for d in order:
-                if d < 8:
-                    back(wave, d).start()
-        mine = pltpu.make_async_copy(houts[wave].at[rows_of(plane)], back_view(wave, plane), local_sem.at[2])
-        mine.start()
-        mine.wait()
+    def attention(wave, group):
+        order = range(4 * group + 1, 4 * group + 5)
+        for d in order:
+            attend(wave, d)
+        for d in order:
+            if d < 8:
+                back(wave, d).start()
+            else:
+                mine = pltpu.make_async_copy(houts[wave].at[rows_of(plane)], back_view(wave, plane), local_sem.at[2])
+                mine.start()
+                mine.wait()
 
     def back_receive(wave):
         for d in range(1, 8):
@@ -415,27 +435,31 @@
         for half in HALVES:
             gh[wave].begin(half)
 
+    def near(gather, half):
+        for role in (BP, BM, A):
+            gather.arrive(role, half)
+
+    complete(0)
     mine0 = attend_send(0)
+    complete(1)
+    attend_receive(0, mine0)
     mine1 = attend_send(1)
-    attend_receive(0, mine0)
-    attention(0)
+    attention(0, 0)
+    attention(0, 1)
     back_receive(0)
     attend_receive(1, mine1)
     for half in HALVES:
         go.begin(half)
-    attention(1)
+    attention(1, 0)
+    near(gh[0], 0)
+    attention(1, 1)
+    near(gh[0], 1)
     back_receive(1)
 
-    def near(gather, half):
-        for role in (BP, BM, A):
-            gather.arrive(role, half)
-
-    near(gh[0], 0)
-    near(go, 0)
-    near(gh[0], 1)
-    near(go, 1)
     gh[0].arrive(D, 0)
     gh[0].arrive(D, 1)
+    near(go, 0)
+    near(go, 1)
     near(gh[1], 0)
     for half in HALVES:
         go.arrive(CP, half)
@@ -515,7 +539,7 @@
             pltpu.VMEM((tokens, heads // 2), bf16),
             pltpu.VMEM((tokens, ocols), f32),
             pltpu.VMEM((rows, 8, padded), f32),
-            pltpu.VMEM((padded, 128), f32),
+            pltpu.VMEM((2, padded, 128), f32),
             *pairs, *pairs, *pairs, *pairs, *pairs, *pairs, *pairs,
             dma((2, 8)), dma((2, 8)), dma((2, 8)), dma((2, 8)), dma((2, 8)), dma((2, 8)),
             dma((8,)), dma((8,)), dma((4,)),

time: 181 us -> 161 us (0.89)
  Pallas kernels: 179 us -> 159 us
    pallas_call x1, Pallas kernels: 179 us -> 159 us  [local(): pl.pallas_call(block_kernel, out_shape=jax.ShapeDtypeStruct((tokens, feat...]
where the time goes in v3:
time: 161 us
  Pallas kernels  159 us (99%)
  local copies, waits for them, and re-layouts  2.04 us (1%)
    pallas_call x1, Pallas kernels, local(): pl.pallas_call(block_kernel, out_shape=jax.ShapeDtypeStruct((tokens, feat...  159 us

profile of v3, /device:TPU:1, one launch (start us, length us, event | category | flops | bytes accessed | tf_op | source)
XLA Modules:
  0.0 160.7 jit_solution(615541035370305622)
XLA Ops:
  0.0 158.6 %attention_block.1 = bf16[576,640]{1,0:T(8,128)(2,1)} custom-call(bf16[576,640]{1,0:T(8,128)(2,1)} %bitcast.5, f32[1,5120]{1,0:T(1,128)} %bitcast.6, f32[1,5120]{1,0:T(1,128)} %bitcast.7, bf16[320,1536]{1,0:T(8,128)(2,1)} %wq_ref.1, bf16[256,640]{1,0:T(8,128)(2,1)} %wo_ref.1), custom_call_target="tpu_custom_call" | custom-call | tf_op jit(solution)/shard_map/attention_block/pallas_call | solution.py:522
  158.6 2.0 %copy.7 = bf16[4,144,640]{2,1,0:T(8,128)(2,1)} copy(bf16[4,144,640]{2,1,0:T(8,128)(2,1)} %bitcast.4) | data formatting | bytes 1474560

commit v4 on v3

--- a/solution.py
+++ b/solution.py
@@ -312,9 +312,9 @@
         gw.shared(role)
         place = gw.place(role)
 
-        @pl.loop(0, wcols // per_head)
+        @pl.loop(0, wcols // 256)
         def _(j):
-            columns = pl.ds(pl.multiple_of(j * per_head, 128), per_head)
+            columns = pl.ds(pl.multiple_of(j * 256, 256), 256)
             if first:
                 acc[:, columns] = product(place, columns)
             else:
@@ -331,6 +331,8 @@
     gw.arrive(CP, 1)
     gw.arrive(CM, 1)
     gw.arrive(E, 1)
+    for half in HALVES:
+        go.begin_across(half)
     for role in (CP, CM, E):
         gw.shared(role)
 
@@ -446,30 +448,31 @@
     mine1 = attend_send(1)
     attention(0, 0)
     attention(0, 1)
+    for half in HALVES:
+        go.begin_ring(half)
     back_receive(0)
     attend_receive(1, mine1)
-    for half in HALVES:
-        go.begin(half)
     attention(1, 0)
     near(gh[0], 0)
+    near(go, 0)
+    near(go, 1)
     attention(1, 1)
     near(gh[0], 1)
-    back_receive(1)
-
     gh[0].arrive(D, 0)
     gh[0].arrive(D, 1)
-    near(go, 0)
-    near(go, 1)
-    near(gh[1], 0)
+    back_receive(1)
+
     for half in HALVES:
         go.arrive(CP, half)
         go.arrive(CM, half)
+    for half in HALVES:
+        go.arrive(D, half)
+    near(gh[1], 0)
     near(gh[1], 1)
+    for half in HALVES:
+        go.arrive(E, half)
     gh[1].arrive(D, 0)
     gh[1].arrive(D, 1)
-    for role in (D, E):
-        for half in HALVES:
-            go.arrive(role, half)
     for role in range(8):
         go.shared(role)
 

time: 161 us -> 158 us (0.981); the launches traced: 161 us -> 155 us
  Pallas kernels: 159 us -> 153 us
    pallas_call x1, Pallas kernels: 159 us -> 153 us  [local(): pl.pallas_call(block_kernel, out_shape=jax.ShapeDtypeStruct((tokens, feat...]
where the time goes in v4:
time: 158 us; the launch traced here: 155 us
  Pallas kernels  153 us (97%)
  local copies, waits for them, and re-layouts  2.04 us (1%)
    pallas_call x1, Pallas kernels, local(): pl.pallas_call(block_kernel, out_shape=jax.ShapeDtypeStruct((tokens, feat...  153 us

profile of v4, /device:TPU:1, one launch (start us, length us, event | category | flops | bytes accessed | tf_op | source)
XLA Modules:
  0.0 155.1 jit_solution(7009616517423422887)
XLA Ops:
  0.0 153.1 %attention_block.1 = bf16[576,640]{1,0:T(8,128)(2,1)} custom-call(bf16[576,640]{1,0:T(8,128)(2,1)} %bitcast.5, f32[1,5120]{1,0:T(1,128)} %bitcast.6, f32[1,5120]{1,0:T(1,128)} %bitcast.7, bf16[320,1536]{1,0:T(8,128)(2,1)} %wq_ref.1, bf16[256,640]{1,0:T(8,128)(2,1)} %wo_ref.1), custom_call_target="tpu_custom_call" | custom-call | tf_op jit(solution)/shard_map/attention_block/pallas_call | solution.py:525
  153.1 2.0 %copy.7 = bf16[4,144,640]{2,1,0:T(8,128)(2,1)} copy(bf16[4,144,640]{2,1,0:T(8,128)(2,1)} %bitcast.4) | data formatting | bytes 1474560

commit v5 on v4

--- a/solution.py
+++ b/solution.py
@@ -348,19 +348,17 @@
 
     attending = []
 
-    def complete(wave):
-        for z in range(2):
-            columns = pl.ds((z * 2 + wave) * per_head, per_head)
-            total = acc[:, columns]
-            for role in (CP, CM, E):
-                total += product(gw.place(role), columns)
-            qkv[:, columns] = total.astype(jnp.bfloat16)
-
-    def attend_send(wave):
-        src, dst, _ = to_attend(wave, 0)
-        mine = pltpu.make_async_copy(src, dst, local_sem.at[wave])
-        mine.start()
-        for d in range(1, 8):
+    across_first = (1, 3, 5, 7, 2, 4, 6)
+
+    def complete(wave, z):
+        columns = pl.ds(pl.multiple_of((z * 2 + wave) * per_head, 128), per_head)
+        total = acc[:, columns]
+        for role in (CP, CM, E):
+            total += product(gw.place(role), columns)
+        qkv[:, columns] = total.astype(jnp.bfloat16)
+
+    def attend_send(wave, distances):
+        for d in distances:
             src, dst, device = to_attend(wave, d)
             copy = pltpu.make_async_remote_copy(
                 src_ref=src, dst_ref=dst, send_sem=as_.at[wave, d], recv_sem=ar.at[wave, d],
@@ -368,6 +366,11 @@
             )
             copy.start()
             attending.append(copy)
+
+    def attend_keep(wave):
+        src, dst, _ = to_attend(wave, 0)
+        mine = pltpu.make_async_copy(src, dst, local_sem.at[wave])
+        mine.start()
         return mine
 
     both = pl.ds(HDIM, 2 * HDIM)
@@ -385,7 +388,7 @@
     def attend_receive(wave, mine):
         mine.wait()
         keys_share(wave, 0)
-        for d in range(1, 8):
+        for d in across_first:
             here = items[wave].at[rows_of(lax.rem(plane - d + 8, 8)), pl.ds(0, per_head)]
             pltpu.make_async_copy(here, here, ar.at[wave, d]).wait()
             keys_share(wave, d)
@@ -441,11 +444,16 @@
         for role in (BP, BM, A):
             gather.arrive(role, half)
 
-    complete(0)
-    mine0 = attend_send(0)
-    complete(1)
+    complete(0, 1 - zl)
+    attend_send(0, (1, 3, 5, 7))
+    complete(0, zl)
+    attend_send(0, (2, 4, 6))
+    mine0 = attend_keep(0)
+    complete(1, 1 - zl)
+    complete(1, zl)
     attend_receive(0, mine0)
-    mine1 = attend_send(1)
+    attend_send(1, across_first)
+    mine1 = attend_keep(1)
     attention(0, 0)
     attention(0, 1)
     for half in HALVES:

time: 158 us -> 157 us (level); the launches traced: 155 us -> 156 us
  no operation moved by 1% of the time
where the time goes in v5:
time: 157 us; the launch traced here: 156 us
  Pallas kernels  154 us (98%)
  local copies, waits for them, and re-layouts  2.04 us (1%)
    pallas_call x1, Pallas kernels, local(): pl.pallas_call(block_kernel, out_shape=jax.ShapeDtypeStruct((tokens, feat...  154 us

profile of v5, /device:TPU:1, one launch (start us, length us, event | category | flops | bytes accessed | tf_op | source)
XLA Modules:
  0.0 156.0 jit_solution(7492993690117204824)
XLA Ops:
  0.0 154.0 %attention_block.1 = bf16[576,640]{1,0:T(8,128)(2,1)} custom-call(bf16[576,640]{1,0:T(8,128)(2,1)} %bitcast.5, f32[1,5120]{1,0:T(1,128)} %bitcast.6, f32[1,5120]{1,0:T(1,128)} %bitcast.7, bf16[320,1536]{1,0:T(8,128)(2,1)} %wq_ref.1, bf16[256,640]{1,0:T(8,128)(2,1)} %wo_ref.1), custom_call_target="tpu_custom_call" | custom-call | tf_op jit(solution)/shard_map/attention_block/pallas_call | solution.py:533
  154.0 2.0 %copy.7 = bf16[4,144,640]{2,1,0:T(8,128)(2,1)} copy(bf16[4,144,640]{2,1,0:T(8,128)(2,1)} %bitcast.4) | data formatting | bytes 1474560
